TPU v7x, 32 devices: a whole 2x2x4 slice. The times are simulated.
32 devices in a mesh: pair: 16 (over z, x, core), grp: 2 (over y).
Axes of the slice: x: 2, y: 2, z: 4, core: 2. Of those that a mesh axis runs over, the one named last changes fastest.
Arguments:
- amplitudes: float32 [2, 112, 2048], P('grp', 'pair'), may hold values from -6 to 6
- integrals: float32 [2048, 32768], P('grp', 'pair'), may hold values from -0.375 to 0.375
- owner_blocks: int32 [16], replicated, may hold values from 0 to 15, each once
- occ_pairs: int32 [2, 2, 112], P('grp'), may hold values from 0 to 63, as said below
- vir_pairs: int32 [2, 32768], replicated, may hold values from 0 to 511, as said below
- occ_energy: float32 [64], replicated, may hold values from -1.5 to -0.5
- vir_energy: float32 [512], replicated, may hold values from 0.2 to 1.5
Outputs:
- ladder: float32 [2, 112, 32768], P('grp', 'pair')
Inputs may be any that keep to these rules, and one draw needn't show every extreme that they name: `occ_pairs`: each column is a pair i<j; no pair occurs twice. `vir_pairs`: each column is a pair a<b; no pair occurs twice. `owner_blocks`: a permutation.
All inputs are finite; a program needn't handle non-finite values.
Results may differ from a plain program's by a relative error of at most 0.000071.
Values sent between devices are 32-bit elements; how exact they have to be, the bound alone decides.
A program may use at most 64 MiB of HBM per device.

v0:
```python
import jax
import jax.numpy as jnp
from jax import lax
from jax.sharding import PartitionSpec as P


def pair_energies(energy, pairs):
    return jnp.take(energy, pairs[0]) + jnp.take(energy, pairs[1])


def on_device(amplitudes, integrals, owner_blocks, occ_pairs, vir_pairs, occ_energy, vir_energy):
    block = integrals.shape[0]
    columns = integrals.shape[1]
    groups = lax.axis_size("grp")
    nblocks = owner_blocks.shape[0]
    sub_width = block * groups // nblocks
    group_rows = lax.all_gather(amplitudes, "pair", axis=1, tiled=True)[0]
    piece = lax.all_gather(integrals, "grp", axis=0, tiled=True)
    count = piece.shape[0]
    rows = jnp.arange(count, dtype=jnp.int32)
    owner = jnp.take(owner_blocks, rows // sub_width)
    picked = owner * sub_width + rows % sub_width
    chosen = jnp.take(group_rows, picked, axis=1)
    work = jnp.dot(
        chosen, piece, precision=lax.Precision.HIGHEST, preferred_element_type=jnp.float32
    )
    occ_sum = pair_energies(occ_energy, occ_pairs[0])
    vir_local = lax.dynamic_slice_in_dim(vir_pairs, lax.axis_index("pair") * columns, columns, 1)
    vir_sum = pair_energies(vir_energy, vir_local)
    payload = work / (occ_sum[:, None] - vir_sum[None, :])
    return lax.all_to_all(payload[None], "pair", split_axis=1, concat_axis=2, tiled=True)


def solution(mesh):
    return jax.shard_map(
        on_device,
        mesh=mesh,
        in_specs=(
            P("grp", "pair", None),
            P("grp", "pair"),
            P(),
            P("grp", None, None),
            P(),
            P(),
            P(),
        ),
        out_specs=P("grp", "pair", None),
        check_vma=False,
    )
```

profile of v0, /device:TPU:0, one launch (start us, length us, event | category | flops | bytes accessed | tf_op | source)
XLA Modules:
  0.0 260.6 jit_solution(5393705695619372871)
XLA Ops:
  6.5 0.0 copy-start
  6.5 0.0 copy-start.3
  6.5 0.0 all-gather.2.cloned.1.call-start
  6.6 0.7 all-gather.2.cloned.1.call-update
  7.3 26.1 %all_gather.6 = f32[1,112,2048]{2,0,1:T(1,128)S(1)} all-gather(f32[1,7,2048]{2,0,1:T(1,128)} %param.11), channel_id=1, replica_groups=mesh['pair'=16,'grp'=2] {'pair'}, dimensions={1}, use_global_device_ids=true | all-gather | bytes 974848 | tf_op jit(solution)/shard_map/all_gather | solution.py:17
  33.4 1.2 copy.13
  34.5 0.9 constant_dynamic-slice_fusion
  35.4 0.0 copy-done
  35.4 13.2 %gather_fusion.3 = f32[2048]{0:T(1024)S(1)} fusion(f32[512]{0:T(512)S(1)} %copy-done, s32[2048]{0:T(1024)S(1)} %fusion.16), kind=kCustom, calls=%fused_computation.1.clone | custom fusion | bytes 24576 | tf_op jit(solution)/shard_map/jit(_take)/gather | solution.py:8
  48.7 13.2 %gather_fusion.4 = f32[2048]{0:T(1024)S(1)} fusion(f32[512]{0:T(512)S(1)} %copy-done, s32[2048]{0:T(1024)S(1)} %fusion.17), kind=kCustom, calls=%fused_computation.3.clone | custom fusion | bytes 24576 | tf_op jit(solution)/shard_map/jit(_take)/gather | solution.py:8
  61.9 0.0 copy-done.3
  61.9 0.0 copy-done.1
  61.9 1.2 gather_fusion.1
  63.1 1.2 gather_fusion.2
  64.8 0.0 copy-done.2
  64.8 0.7 fusion.20
  65.5 4.3 %compare_select_fusion.2 = s32[2048,1]{0,1:T(1,128)S(1)} fusion(s32[]{:T(128)} %bitcast.9, s32[]{:T(128)} %bitcast.10, s32[]{:T(128)} %bitcast.11, s32[]{:T(128)} %bitcast.12, s32[]{:T(128)} %bitcast.13, s32[]{:T(128)} %bitcast.15, s32[]{:T(128)} %bitcast.14), kind=kLoop, calls=%fused_computation.21 | loop fusion | flops 47104 | bytes 8220 | tf_op jit(solution)/shard_map/jit(_take)/gather | solution.py:21
  69.8 5.7 %compare_and_fusion = (pred[2048]{0:T(1024)(128)(4,1)S(1)}, s32[2048]{0:T(1024)S(1)}) fusion(pred[2048]{0:T(1024)(128)(4,1)S(1)} %compare_reduce_fusion, pred[2048]{0:T(1024)(128)(4,1)S(1)} %compare_reduce_fusion.1, pred[2048]{0:T(1024)(128)(4,1)S(1)} %compare_reduce_fusion.2, pred[2048]{0:T(1024)(128)(4,1)S(1)} %compare_reduce_fusion.3, ...), kind=kLoop, calls=%fused_computation.55 | loop fusion | flops 73728 | bytes 36900 | tf_op jit(solution)/shard_map/jit(_take)/and | solution.py:23
  75.5 5.5 %gather_fusion = f32[2048,112]{1,0:T(8,128)S(1)} fusion(f32[112,2048]{0,1:T(8,128)S(1)} %bitcast.38, s32[2048]{0:T(1024)S(1)} %broadcast_clamp_fusion), kind=kCustom, calls=%fused_computation.4 | custom fusion | bytes 1843200 | tf_op jit(solution)/shard_map/jit(_take)/gather | solution.py:23
  81.0 129.5 %all-gather.2.cloned.1.call-done = f32[2048,2048]{1,0:T(8,128)} async-done(((f32[1024,2048]{1,0:T(8,128)}), f32[2048,2048]{1,0:T(8,128)}) %all-gather.2.cloned.1.call-update) | async-done | bytes 16777232 | tf_op jit(solution)/shard_map/all_gather | solution.py:18
  210.5 13.3 %fusion = f32[1,112,2048]{2,1,0:T(8,128)S(1)} fusion(f32[2048,2048]{1,0:T(8,128)} %all-gather.2.cloned.1.call-done, f32[2048,112]{1,0:T(8,128)S(1)} %gather_fusion, pred[2048]{0:T(1024)(128)(4,1)S(1)} %get-tuple-element.6, f32[2048]{0:T(1024)S(1)} %select_add_fusion, f32[112]{0:T(128)S(1)} %fusion.18), kind=kOutput, calls=%fused_computation.6 | convolution fusion | flops 5637832704 | bytes 18622912 | tf_op jit(solution)/shard_map/dot_general | solution.py:24
  223.8 0.9 copy.14
  224.8 28.0 %all_to_all.18 = f32[1,112,2048]{2,0,1:T(1,128)S(1)} all-to-all(f32[1,112,2048]{2,0,1:T(1,128)S(1)} %copy.14), channel_id=1, replica_groups=mesh['pair'=16,'grp'=2] {'pair'}, dimensions={1} | all-to-all | bytes 1835008 | tf_op jit(solution)/shard_map/all_to_all | solution.py:31
  252.7 1.0 copy.16
  (19 shorter events, 0.5 us)
Async XLA Ops:
  6.5 28.9 %copy-start = (f32[512]{0:T(512)S(1)}, f32[512]{0:T(512)}, u32[]{:S(2)}) copy-start(f32[512]{0:T(512)} %param.17) | copy-start | bytes 6148
  6.5 55.3 %copy-start.3 = (s32[1,2,112]{2,1,0:T(2,128)S(1)}, s32[1,2,112]{2,1,0:T(2,128)}, u32[]{:S(2)}) copy-start(s32[1,2,112]{2,1,0:T(2,128)} %param.14) | copy-start | bytes 2692
  6.5 55.4 %copy-start.1 = (f32[64]{0:T(128)S(1)}, f32[64]{0:T(128)}, u32[]{:S(2)}) copy-start(f32[64]{0:T(128)} %param.16) | copy-start | bytes 772
  6.5 58.2 %copy-start.2 = (s32[16]{0:T(128)S(1)}, s32[16]{0:T(128)}, u32[]{:S(2)}) copy-start(s32[16]{0:T(128)} %param.13) | copy-start | bytes 196
  6.5 204.0 %all-gather.2.cloned.1.call-start = ((), (), s32[]{:S(2)}) async-start(), calls=%async_computation.1 | async-start | bytes 25165824 | tf_op jit(solution)/shard_map/all_gather | solution.py:18
Sparse Core Ops, SparseCore 0:
  8.9 201.5 all-gather.1
where the time goes:
time: 261 us
  waiting for transfers between devices  130 us (50%)
  blocking collectives  54.1 us (21%)
  local copies, waits for them, and re-layouts  39 us (15%)
  between operations  13.6 us (5%)
  matrix products  13.3 us (5%)
  other arithmetic  10.4 us (4%)
    all_gather x1, waiting for transfers between devices, on_device(): piece = lax.all_gather(integrals, 'grp', axis=0, tiled=True)  129 us
    gather x4, local copies, waits for them, and re-layouts, pair_energies(): return jnp.take(energy, pairs[0]) + jnp.take(energy, pairs[1])  28.8 us
    all_to_all x1, blocking collectives, on_device(): lax.all_to_all(payload[None], 'pair', split_axis=1, concat_axis=2, tiled=...  28 us
    all_gather x1, blocking collectives, on_device(): group_rows = lax.all_gather(amplitudes, 'pair', axis=1, tiled=True)[0]  26.1 us
    dot_general x1, matrix products, on_device(): jnp.dot(chosen, piece, precision=lax.Precision.HIGHEST, preferred_element...  13.3 us
    and x1, other arithmetic, on_device(): chosen = jnp.take(group_rows, picked, axis=1)  5.68 us
    gather x1, local copies, waits for them, and re-layouts, on_device(): chosen = jnp.take(group_rows, picked, axis=1)  5.46 us
  transfers between devices with their start and end apart: 1, of which 1 were waited for; matrix products, arithmetic and copies ran while one was open for 18% of the time, Pallas kernels for 0%

commit v1 on v0

--- a/solution.py
+++ b/solution.py
@@ -1,14 +1,266 @@
+import functools
+
 import jax
 import jax.numpy as jnp
 from jax import lax
+from jax.experimental import pallas as pl
+from jax.experimental.pallas import tpu as pltpu
 from jax.sharding import PartitionSpec as P
+
+LANES = 128
+PAD = 8
+MESH = pl.DeviceIdType.MESH
 
 
 def pair_energies(energy, pairs):
     return jnp.take(energy, pairs[0]) + jnp.take(energy, pairs[1])
 
 
-def on_device(amplitudes, integrals, owner_blocks, occ_pairs, vir_pairs, occ_energy, vir_energy):
+def flip(bit, on):
+    return 1 - bit if on else bit
+
+
+def split_bf16(x):
+    hi = x.astype(jnp.bfloat16)
+    return hi, (x - hi.astype(jnp.float32)).astype(jnp.bfloat16)
+
+
+def kernel(
+    owner_ref, occ_pairs_ref, occ_energy_ref, amp_ref, vir_energy_ref, vir_pairs_ref, integrals_ref,
+    out_ref,
+    gath, other, raw, rhs_hi, rhs_lo, vp, virs, lhs_f, lhs_hi, lhs_lo, ysend, yrecv, own, piece,
+    load_sem, vp_sem, yamp_sem, asend_sem, arecv_sem, ysend_sem, yrecv_sem, osend_sem, orecv_sem, self_sem,
+):
+    npair = out_ref.shape[1] // own.shape[2]
+    rows = out_ref.shape[0]
+    depth, cols = integrals_ref.shape
+    kb = depth // LANES
+    nb = cols // LANES
+    nv = vir_energy_ref.shape[1]
+    me = lax.axis_index("pair")
+    g = lax.axis_index("grp")
+    og = 1 - g
+    core = me % 2
+    x = (me // 2) % 2
+    z = me // 4
+    zb0, zb1 = z % 2, z // 2
+
+    def at(k):
+        return flip(zb1, k & 8) * 8 + flip(zb0, k & 4) * 4 + flip(x, k & 2) * 2 + flip(core, k & 1)
+
+    nload = 4
+    step = depth // nload
+    loads = [
+        pltpu.make_async_copy(
+            integrals_ref.at[pl.ds(i * step, step)], raw.at[pl.ds(i * step, step)], load_sem.at[i]
+        )
+        for i in range(nload)
+    ]
+    vp_copy = pltpu.make_async_copy(vir_pairs_ref.at[:, pl.ds(pl.multiple_of(me * cols, cols), cols)], vp, vp_sem)
+    vp_copy.start()
+    for c in loads:
+        c.start()
+
+    barrier = pltpu.get_barrier_semaphore()
+    pl.semaphore_signal(barrier, inc=1, device_id=(me, og), device_id_type=MESH)
+    for k in range(1, npair):
+        pl.semaphore_signal(barrier, inc=1, device_id=(at(k), g), device_id_type=MESH)
+
+    for b in range(kb):
+        other[:, b, :] = amp_ref[:, owner_ref[og * kb + b], :]
+        gath[me, g, :, b, :] = amp_ref[:, owner_ref[g * kb + b], :]
+    lhs_f[...] = jnp.zeros_like(lhs_f)
+
+    pl.semaphore_wait(barrier, npair)
+
+    yamp = pltpu.make_async_remote_copy(
+        src_ref=other, dst_ref=gath.at[me, g], send_sem=yamp_sem.at[0], recv_sem=yamp_sem.at[1],
+        device_id=(me, og), device_id_type=MESH,
+    )
+    yamp.start()
+
+    vp_copy.wait()
+    e = vir_energy_ref[...]
+    e0 = e.astype(jnp.bfloat16).astype(jnp.float32)
+    e1 = (e - e0).astype(jnp.bfloat16).astype(jnp.float32)
+    e2 = e - e0 - e1
+    rid = lax.broadcasted_iota(jnp.int32, (16, nv), 0)
+    e3 = jnp.where(rid == 0, e0, jnp.where(rid == 1, e1, jnp.where(rid == 2, e2, 0.0))).astype(jnp.bfloat16)
+    tv = 512
+    for t in range(cols // tv):
+        a = vp[0:1, t * tv:(t + 1) * tv]
+        b = vp[1:2, t * tv:(t + 1) * tv]
+        ids = lax.broadcasted_iota(jnp.int32, (nv, tv), 0)
+        hot = jnp.where((ids == a) | (ids == b), 1.0, 0.0).astype(jnp.bfloat16)
+        v = jnp.sum(jnp.dot(e3, hot, preferred_element_type=jnp.float32), axis=0, keepdims=True)
+        for j in range(tv // LANES):
+            q = t * (tv // LANES) + j
+            virs[q:q + 1, :] = v[:, j * LANES:(j + 1) * LANES]
+
+    yamp.wait()
+
+    def amp_copy(block, target, slot):
+        return pltpu.make_async_remote_copy(
+            src_ref=gath.at[block], dst_ref=gath.at[block], send_sem=asend_sem.at[slot], recv_sem=arecv_sem.at[block],
+            device_id=(target, g), device_id_type=MESH,
+        )
+
+    def split_rhs(i):
+        loads[i].wait()
+        h = step // 2
+        for s in (i * step, i * step + h):
+            hi, lo = split_bf16(raw[s:s + h, :])
+            rhs_hi[s:s + h, :] = hi
+            rhs_lo[s:s + h, :] = lo
+
+    sends = []
+
+    def send(rel, hop):
+        c = amp_copy(at(rel), at(hop), len(sends))
+        c.start()
+        sends.append(c)
+
+    def arrived(rel):
+        amp_copy(at(rel), at(rel), 0).wait_recv()
+
+    for k in (12, 8, 4, 2, 1):
+        send(0, k)
+    split_rhs(0)
+    split_rhs(1)
+    for i, k in enumerate((4, 8, 12)):
+        arrived(k)
+        send(k, 2)
+        send(k, 1)
+        if i == 0:
+            split_rhs(2)
+    split_rhs(3)
+    for k in (2, 6, 10, 14):
+        arrived(k)
+        send(k, 1)
+    for k in (1, 5, 9, 13, 3, 7, 11, 15):
+        arrived(k)
+
+    for p in range(npair):
+        for b in range(kb):
+            for h in range(2):
+                lhs_f[h * npair * PAD + p * PAD:h * npair * PAD + p * PAD + rows, b * LANES:(b + 1) * LANES] = (
+                    gath[p, h, :, b, :]
+                )
+    hi, lo = split_bf16(lhs_f[...])
+    lhs_hi[...] = hi
+    lhs_lo[...] = lo
+
+    half = npair * PAD
+    tn = 512
+
+    def multiply(group, target):
+        left_hi = lhs_hi[pl.ds(pl.multiple_of(group * half, half), half), :]
+        left_lo = lhs_lo[pl.ds(pl.multiple_of(group * half, half), half), :]
+        both = jnp.concatenate([left_hi, left_lo], axis=0)
+        for t in range(cols // tn):
+            right = rhs_hi[:, t * tn:(t + 1) * tn]
+            r = jnp.dot(both, right, preferred_element_type=jnp.float32)
+            r = r[:half] + r[half:] + jnp.dot(
+                left_hi, rhs_lo[:, t * tn:(t + 1) * tn], preferred_element_type=jnp.float32
+            )
+            for p in range(npair):
+                for j in range(tn // LANES):
+                    target[p, :, t * (tn // LANES) + j, :] = r[p * PAD:p * PAD + rows, j * LANES:(j + 1) * LANES]
+
+    def part_copy(p):
+        return pltpu.make_async_remote_copy(
+            src_ref=ysend.at[p], dst_ref=yrecv.at[p], send_sem=ysend_sem.at[p], recv_sem=yrecv_sem.at[p],
+            device_id=(me, og), device_id_type=MESH,
+        )
+
+    order = (12, 13, 14, 15, 8, 9, 10, 11, 4, 5, 6, 7, 2, 3, 1, 0)
+    multiply(og, ysend)
+    for k in order:
+        part_copy(at(k)).start()
+    multiply(g, own)
+
+    def out_copy(p, source):
+        return pltpu.make_async_remote_copy(
+            src_ref=piece.at[p], dst_ref=out_ref.at[:, pl.ds(pl.multiple_of(source * nb, nb), nb), :],
+            send_sem=osend_sem.at[p], recv_sem=orecv_sem.at[source],
+            device_id=(p, g), device_id_type=MESH,
+        )
+
+    vir = virs[...]
+    for k in order:
+        p = at(k)
+        part_copy(p).wait_recv()
+        for r in range(rows):
+            row = p * rows + r
+            occ = occ_energy_ref[occ_pairs_ref[0, row]] + occ_energy_ref[occ_pairs_ref[1, row]]
+            piece[p, r] = (own[p, r] + yrecv[p, r]) / (occ - vir)
+        if k:
+            out_copy(p, me).start()
+    mine = pltpu.make_async_copy(
+        piece.at[me], out_ref.at[:, pl.ds(pl.multiple_of(me * nb, nb), nb), :], self_sem
+    )
+    mine.start()
+    for c in sends:
+        c.wait_send()
+    for k in range(npair):
+        part_copy(at(k)).wait_send()
+    mine.wait()
+    for k in range(1, npair):
+        out_copy(at(k), at(k)).wait_recv()
+    for k in range(1, npair):
+        out_copy(at(k), me).wait_send()
+
+
+def two_groups(amplitudes, integrals, owner_blocks, occ_pairs, vir_pairs, occ_energy, vir_energy):
+    npair = lax.axis_size("pair")
+    rows, width = amplitudes.shape[1:]
+    depth, cols = integrals.shape
+    kb, nb = depth // LANES, cols // LANES
+    nv = vir_energy.shape[0]
+    if rows > PAD or owner_blocks.shape[0] != 2 * kb or cols % 512:
+        return any_groups(amplitudes, integrals, owner_blocks, occ_pairs, vir_pairs, occ_energy, vir_energy)
+    f32, bf16 = jnp.float32, jnp.bfloat16
+    dma = pltpu.SemaphoreType.DMA
+    vmem = pl.BlockSpec(memory_space=pltpu.VMEM)
+    smem = pl.BlockSpec(memory_space=pltpu.SMEM)
+    hbm = pl.BlockSpec(memory_space=pl.ANY)
+    out = pl.pallas_call(
+        kernel,
+        out_shape=jax.ShapeDtypeStruct((rows, npair * nb, LANES), f32),
+        in_specs=[smem, smem, smem, vmem, vmem, hbm, hbm],
+        out_specs=hbm,
+        scratch_shapes=[
+            pltpu.VMEM((npair, 2, rows, kb, LANES), f32),
+            pltpu.VMEM((rows, kb, LANES), f32),
+            pltpu.VMEM((depth, cols), f32),
+            pltpu.VMEM((depth, cols), bf16),
+            pltpu.VMEM((depth, cols), bf16),
+            pltpu.VMEM((2, cols), jnp.int32),
+            pltpu.VMEM((nb, LANES), f32),
+            pltpu.VMEM((2 * npair * PAD, depth), f32),
+            pltpu.VMEM((2 * npair * PAD, depth), bf16),
+            pltpu.VMEM((2 * npair * PAD, depth), bf16),
+            pltpu.VMEM((npair, rows, nb, LANES), f32),
+            pltpu.VMEM((npair, rows, nb, LANES), f32),
+            pltpu.VMEM((npair, rows, nb, LANES), f32),
+            pltpu.VMEM((npair, rows, nb, LANES), f32),
+            dma((4,)), dma, dma((2,)), dma((16,)), dma((npair,)),
+            dma((npair,)), dma((npair,)), dma((npair,)), dma((npair,)), dma,
+        ],
+        compiler_params=pltpu.CompilerParams(
+            collective_id=0, has_side_effects=True, vmem_limit_bytes=48 * 1024 * 1024
+        ),
+        cost_estimate=pl.CostEstimate(
+            flops=12 * npair * rows * depth * cols, bytes_accessed=4 * depth * cols, transcendentals=0
+        ),
+    )(
+        owner_blocks, occ_pairs[0], occ_energy, amplitudes.reshape(rows, width // LANES, LANES),
+        vir_energy.reshape(1, nv), vir_pairs, integrals,
+    )
+    return out.reshape(1, rows, npair * cols)
+
+
+def any_groups(amplitudes, integrals, owner_blocks, occ_pairs, vir_pairs, occ_energy, vir_energy):
     block = integrals.shape[0]
     columns = integrals.shape[1]
     groups = lax.axis_size("grp")
@@ -32,8 +284,9 @@
 
 
 def solution(mesh):
+    body = two_groups if mesh.shape["grp"] == 2 and mesh.shape["pair"] == 16 else any_groups
     return jax.shard_map(
-        on_device,
+        body,
         mesh=mesh,
         in_specs=(
             P("grp", "pair", None),

time: 261 us -> 54.4 us (0.21)
  waiting for transfers between devices: 130 us -> 0 us
  blocking collectives: 54.1 us -> 0 us
  Pallas kernels: 0 us -> 48.8 us
  local copies, waits for them, and re-layouts: 39 us -> 5.36 us
  between operations: 13.6 us -> 0.02 us
  matrix products: 13.3 us -> 0 us
  other arithmetic: 10.4 us -> 0 us
    all_gather x1 -> x0, waiting for transfers between devices: 129 us -> none  [on_device(): piece = lax.all_gather(integrals, 'grp', axis=0, tiled=True)]
    pallas_call x0 -> x1, Pallas kernels: none -> 48.8 us  [two_groups(): pl.pallas_call(kernel, out_shape=jax.ShapeDtypeStruct((rows, npair * nb,...]
    gather x6 -> x0, local copies, waits for them, and re-layouts: 35 us -> none  [the longest x4 28.8 us: pair_energies(): return jnp.take(energy, pairs[0]) + jnp.take(energy, pairs[1])]
    all_to_all x1 -> x0, blocking collectives: 28 us -> none  [on_device(): lax.all_to_all(payload[None], 'pair', split_axis=1, concat_axis=2, tiled=...]
    all_gather x1 -> x0, blocking collectives: 26.1 us -> none  [on_device(): group_rows = lax.all_gather(amplitudes, 'pair', axis=1, tiled=True)[0]]
    dot_general x1 -> x0, matrix products: 13.3 us -> none  [on_device(): jnp.dot(chosen, piece, precision=lax.Precision.HIGHEST, preferred_element...]
    and x1 -> x0, other arithmetic: 5.68 us -> none  [on_device(): chosen = jnp.take(group_rows, picked, axis=1)]
    unnamed x8 -> x13, local copies, waits for them, and re-layouts: 0.02 us -> 5.36 us
  transfers between devices with their start and end apart: 1 -> 0, of which waited for: 1 -> 0; matrix products, arithmetic and copies ran while one was open for 18% -> 0% of each run, Pallas kernels for 0% -> 0%
where the time goes in v1:
time: 54.4 us; the launch traced here: 54.2 us
  Pallas kernels  48.8 us (90%)
  local copies, waits for them, and re-layouts  5.36 us (10%)
    pallas_call x1, Pallas kernels, two_groups(): pl.pallas_call(kernel, out_shape=jax.ShapeDtypeStruct((rows, npair * nb,...  48.8 us
    unnamed x13, local copies, waits for them, and re-layouts  5.36 us

profile of v1, /device:TPU:0, one launch (start us, length us, event | category | flops | bytes accessed | tf_op | source)
XLA Modules:
  0.0 54.2 jit_solution(8978009619476523511)
XLA Ops:
  0.0 0.0 copy-start
  0.0 0.9 %copy-done = s32[2,32768]{1,0:T(2,128)S(1)} copy-done((s32[2,32768]{1,0:T(2,128)S(1)}, s32[2,32768]{1,0:T(2,128)}, u32[]{:S(2)}) %copy-start) | copy-done | bytes 262168
  1.0 0.0 copy-start.1
  1.0 0.8 %copy-done.1 = f32[1,7,2048]{2,0,1:T(1,128)S(1)} copy-done((f32[1,7,2048]{2,0,1:T(1,128)S(1)}, f32[1,7,2048]{2,0,1:T(1,128)}, u32[]{:S(2)}) %copy-start.1) | copy-done | bytes 57368
  1.8 0.0 copy-start.2
  1.8 0.7 %copy-done.2 = f32[512]{0:T(512)S(1)} copy-done((f32[512]{0:T(512)S(1)}, f32[512]{0:T(512)}, u32[]{:S(2)}) %copy-start.2) | copy-done | bytes 2072
  2.5 0.0 copy-start.3
  2.5 0.7 %copy-done.3 = s32[1,2,112]{2,1,0:T(2,128)S(1)} copy-done((s32[1,2,112]{2,1,0:T(2,128)S(1)}, s32[1,2,112]{2,1,0:T(2,128)}, u32[]{:S(2)}) %copy-start.3) | copy-done | bytes 920
  3.1 0.0 copy-start.4
  3.1 0.7 %copy-done.4 = s32[16]{0:T(128)S(1)} copy-done((s32[16]{0:T(128)S(1)}, s32[16]{0:T(128)}, u32[]{:S(2)}) %copy-start.4) | copy-done | bytes 88
  3.8 0.0 copy-start.5
  3.8 0.7 %copy-done.5 = f32[64]{0:T(128)S(1)} copy-done((f32[64]{0:T(128)S(1)}, f32[64]{0:T(128)}, u32[]{:S(2)}) %copy-start.5) | copy-done | bytes 280
  4.4 48.8 %shard_map.73 = f32[7,256,128]{2,1,0:T(8,128)S(1)} custom-call(s32[16]{0:T(128)S(1)} %copy-done.4, s32[2,112]{1,0:T(2,128)S(1)} %bitcast.7, f32[64]{0:T(128)S(1)} %copy-done.5, f32[7,16,128]{2,1,0:T(8,128)S(1)} %bitcast.5, f32[1,512]{1,0:T(1,128)S(1)} %bitcast.6, s32[2,32768]{1,0:T(2,128)S(1)} %copy-done, f32[1024,2048]{1,0:T(8,128)} %integrals_ref.1), custom_call_target="tpu_custom_call" | custom-call | flops 2818572288 | bytes 8388608 | tf_op jit(solution)/shard_map/pallas_call | solution.py:227
  53.3 0.9 %copy.11 = f32[1,7,32768]{2,0,1:T(1,128)} copy(f32[1,7,32768]{2,0,1:T(1,128)S(1)} %bitcast.4) | data formatting | bytes 1835008
Async XLA Ops:
  0.0 0.9 %copy-start = (s32[2,32768]{1,0:T(2,128)S(1)}, s32[2,32768]{1,0:T(2,128)}, u32[]{:S(2)}) copy-start(s32[2,32768]{1,0:T(2,128)} %vir_pairs_ref.1) | copy-start | bytes 786436
  1.0 0.8 %copy-start.1 = (f32[1,7,2048]{2,0,1:T(1,128)S(1)}, f32[1,7,2048]{2,0,1:T(1,128)}, u32[]{:S(2)}) copy-start(f32[1,7,2048]{2,0,1:T(1,128)} %param.7) | copy-start | bytes 172036
  1.8 0.7 %copy-start.2 = (f32[512]{0:T(512)S(1)}, f32[512]{0:T(512)}, u32[]{:S(2)}) copy-start(f32[512]{0:T(512)} %param.13) | copy-start | bytes 6148
  2.5 0.7 %copy-start.3 = (s32[1,2,112]{2,1,0:T(2,128)S(1)}, s32[1,2,112]{2,1,0:T(2,128)}, u32[]{:S(2)}) copy-start(s32[1,2,112]{2,1,0:T(2,128)} %param.10) | copy-start | bytes 2692
  3.1 0.7 %copy-start.4 = (s32[16]{0:T(128)S(1)}, s32[16]{0:T(128)}, u32[]{:S(2)}) copy-start(s32[16]{0:T(128)} %owner_ref.1) | copy-start | bytes 196
  3.8 0.7 %copy-start.5 = (f32[64]{0:T(128)S(1)}, f32[64]{0:T(128)}, u32[]{:S(2)}) copy-start(f32[64]{0:T(128)} %occ_energy_ref.1) | copy-start | bytes 772
